TPU v7x, 32 devices: a whole 2x2x4 slice. The times are simulated.
32 devices in a mesh: grp: 2 (over y), feat: 4 (over z), tgt: 2 (over x), lay: 2 (over core).
Axes of the slice: x: 2, y: 2, z: 4, core: 2. Of those that a mesh axis runs over, the one named last changes fastest.
Arguments:
- decoder: bfloat16 [2, 32768, 4608], P('lay', 'feat', 'tgt'), may hold values from -6 to 6
- value_weight: bfloat16 [2, 1024, 4608], P('lay', 'feat', 'tgt'), may hold values from -0.09375 to 0.09375
- out_weight: bfloat16 [2, 2048, 4608], P('lay', 'feat', 'tgt'), may hold values from -0.09375 to 0.09375
- target_enc: bfloat16 [2, 512, 4608], P('lay', 'grp', 'tgt'), parts along dimension 1, may hold values from -6 to 6
- target_pos: int32 [2, 512], P('lay', 'grp'), parts along dimension 1, may hold values from 0 to 31
- attention: float32 [2, 32, 32, 32], P('lay', 'grp', 'feat'), parts along dimension 1, may hold values from 0.005 to 0.05
- norm_gain: float32 [2, 3, 4608], P('lay', None, 'tgt'), may hold values from 0.1 to 1.9
- norm_rstd: float32 [2, 6, 32], P('lay', 'grp'), parts along dimension 1, may hold values from 0.5 to 2
- source_owner: int32 [8192, 1], P(('grp', 'feat')), parts along dimension 0, may hold values from 0 to 3; in each aligned block of 1024 rows (0 to 1023, 1024 to 2047, ...) at most 512 rows name the same one
- source_row: int32 [8192], P(('grp', 'feat')), parts along dimension 0, may hold values from 0 to 8191
- source_act: float32 [8192], P(('grp', 'feat')), parts along dimension 0, may hold values from 0.25 to 2
- source_valid: int32 [8192], P(('grp', 'feat')), parts along dimension 0, may hold values 0 or 1
Outputs:
- edges: bfloat16 [2, 512, 4096], P('lay', ('grp', 'tgt'), 'feat'), parts along dimension 1
There are 2 independent parts, one for each index of `grp`. A program takes and returns all parts, laid end to end along the dimension named above; an argument that names none is the same for every part. Nothing has to cross between parts.
Inputs may be any that keep to these rules, and one draw needn't show every extreme that they name: `source_owner`: in each aligned block of 1024 slots (the source slots of one index of feat), no shard is named by more than 512 slots, a bound that some block reaches.
All inputs are finite; a program needn't handle non-finite values. No bound on the sum of `source_valid` on one device may be relied on, other than what follows from the above.
Results may differ from a plain program's by a relative error of at most 0.012.
Values may be sent and summed in bfloat16 or wider, within the bound.
A program may use at most 192 MiB of HBM per device.

v0:
```python
import functools
import jax
import jax.numpy as jnp
from jax import lax
from jax.experimental import pallas as pl
from jax.experimental.pallas import tpu as pltpu
from jax.sharding import PartitionSpec as P

HEADS = 16
KV = 8
HD = 128
K = 128


def gather_kernel(index_ref, shard_ref, out_ref, held, sems):
    step = pl.program_id(0)
    steps = pl.num_programs(0)
    block = out_ref.shape[0]
    width = out_ref.shape[1]

    def fetch(of, slot):
        @pl.loop(0, block, unroll=8)
        def _(i):
            pltpu.make_async_copy(
                shard_ref.at[index_ref[of * block + i] // 8], held.at[slot, i], sems.at[slot]
            ).start()

    @pl.when(step == 0)
    def _():
        fetch(0, 0)

    @pl.when(step + 1 < steps)
    def _():
        fetch(step + 1, (step + 1) % 2)

    now = step % 2
    pltpu.make_async_copy(shard_ref.at[pl.ds(0, block)], held.at[now], sems.at[now]).wait()
    sublane = lax.broadcasted_iota(jnp.int32, (8, width), 0)

    @pl.loop(0, block // 16)
    def _(chunk):
        halves = []
        for half in range(2):
            kept = jnp.zeros((8, width), jnp.float32)
            for u in range(8):
                i = chunk * 16 + half * 8 + u
                row = index_ref[step * block + i] % 8
                group = held[now, i].astype(jnp.float32)
                turned = pltpu.roll(group, (u + 8 - row) % 8, 0)
                kept = jnp.where(sublane == u, turned, kept)
            halves.append(kept)
        out_ref[pl.ds(pl.multiple_of(chunk * 16, 16), 16), :] = jnp.concatenate(
            halves, axis=0
        ).astype(jnp.bfloat16)


def gather_rows(shard, index):
    slots = index.shape[0]
    width = shard.shape[1]
    block = 64
    return pl.pallas_call(
        gather_kernel,
        grid_spec=pltpu.PrefetchScalarGridSpec(
            num_scalar_prefetch=1,
            grid=(slots // block,),
            in_specs=[pl.BlockSpec(memory_space=pl.ANY)],
            out_specs=pl.BlockSpec((block, width), lambda i, index: (i, 0)),
            scratch_shapes=[
                pltpu.VMEM((2, block, 8, width), jnp.bfloat16),
                pltpu.SemaphoreType.DMA((2,)),
            ],
        ),
        out_shape=jax.ShapeDtypeStruct((slots, width), jnp.bfloat16),
        compiler_params=pltpu.CompilerParams(vmem_limit_bytes=24 * 1024 * 1024),
        cost_estimate=pl.CostEstimate(
            flops=slots * width * 16, bytes_accessed=slots * width * 18, transcendentals=0
        ),
    )(index, shard.reshape(shard.shape[0] // 8, 8, width))


def score_kernel(kv_of_block, rows_ref, values_ref, heads_ref, picked_ref, token_ref, out_ref):
    group = HEADS // KV
    projected = lax.dot_general(
        values_ref[...],
        rows_ref[...],
        (((1,), (1,)), ((), ())),
        preferred_element_type=jnp.float32,
    ).astype(jnp.bfloat16)
    tokens = picked_ref.shape[2]
    slots = token_ref.shape[1]
    which = lax.broadcasted_iota(jnp.int32, (tokens, slots), 0) == token_ref[...]
    which = jnp.where(which, 1.0, 0.0).astype(jnp.bfloat16)
    total = jnp.zeros(out_ref.shape, jnp.float32)
    for block in range(KV):
        kv = kv_of_block[block]
        for g in range(group):
            match = jnp.dot(
                heads_ref[kv, :, g * HD : (g + 1) * HD],
                projected[block * HD : (block + 1) * HD],
                preferred_element_type=jnp.float32,
            )
            weight = jnp.dot(
                picked_ref[kv * group + g], which, preferred_element_type=jnp.float32
            )
            total = total + match * weight
    out_ref[...] = total.astype(jnp.bfloat16)


def owner_scores(kv_of_block, rows, values, heads, picked, tokens_of_slot):
    slots, width = rows.shape
    targets = heads.shape[1]
    block = 512
    return pl.pallas_call(
        functools.partial(score_kernel, kv_of_block),
        grid=(slots // block,),
        in_specs=[
            pl.BlockSpec((block, width), lambda i: (i, 0)),
            pl.BlockSpec(values.shape, lambda i: (0, 0)),
            pl.BlockSpec(heads.shape, lambda i: (0, 0, 0)),
            pl.BlockSpec(picked.shape, lambda i: (0, 0, 0)),
            pl.BlockSpec((1, block), lambda i: (0, i)),
        ],
        out_specs=pl.BlockSpec((targets, block), lambda i: (0, i)),
        out_shape=jax.ShapeDtypeStruct((targets, slots), jnp.bfloat16),
        compiler_params=pltpu.CompilerParams(vmem_limit_bytes=48 * 1024 * 1024),
    )(rows, values, heads, picked, tokens_of_slot)


def place_kernel(replies_ref, place_ref, scale_ref, out_ref):
    capacity = replies_ref.shape[2]
    slots = place_ref.shape[1]
    total = jnp.zeros(out_ref.shape, jnp.float32)
    spots = lax.broadcasted_iota(jnp.int32, (capacity, slots), 0)
    for owner in range(replies_ref.shape[0]):
        which = jnp.where(spots + owner * capacity == place_ref[...], 1.0, 0.0)
        total = total + jnp.dot(
            replies_ref[owner], which.astype(jnp.bfloat16), preferred_element_type=jnp.float32
        )
    out_ref[...] = (total * scale_ref[...]).astype(jnp.bfloat16)


def on_device(
    decoder,
    value_weight,
    out_weight,
    target_enc,
    target_pos,
    attention,
    norm_gain,
    norm_rstd,
    source_owner,
    source_row,
    source_act,
    source_valid,
):
    n_feat = lax.axis_size("feat")
    n_tgt = lax.axis_size("tgt")
    me_tgt = lax.axis_index("tgt")
    shard = decoder[0]
    shard_rows = shard.shape[0]
    slot_count = source_row.shape[0]
    capacity = max(2, 2 * slot_count // n_feat)
    gains = norm_gain[0]
    positions = target_pos[0]
    targets = positions.shape[0]
    owners = source_owner[:, 0]

    def shifted(x, step):
        return lax.ppermute(x, "tgt", [(i, (i + step) % n_tgt) for i in range(n_tgt)])

    gained_values = (value_weight[0].astype(jnp.float32) * gains[2]).astype(jnp.bfloat16)
    n_grp = lax.axis_size("grp")
    me_grp = lax.axis_index("grp")
    kv_of_block = list(range(KV))
    whole_heads = gained_values.shape[0] == n_grp * HD and n_grp == 2
    if whole_heads:
        half = lax.dynamic_slice_in_dim(gained_values, me_grp * HD, HD)
        target_enc, half = lax.optimization_barrier((target_enc, half))
        kv_of_block = [n_grp * j + g for g in range(n_grp) for j in range(n_feat)]
        values = lax.all_gather(half, ("grp", "feat"), axis=0, tiled=True)
    else:
        values = lax.all_gather(gained_values, "feat", axis=0, tiled=True)

    member = (owners[:, None] == jnp.arange(n_feat, dtype=jnp.int32)[None, :]).astype(jnp.int32)
    ranks = jnp.sum((jnp.cumsum(member, axis=0) - 1) * member, axis=1)
    flat_slot = owners * capacity + ranks
    token_here = jnp.arange(slot_count, dtype=jnp.int32) // K
    asked = jnp.sum(
        jnp.where(
            flat_slot[None, :] == jnp.arange(n_feat * capacity, dtype=jnp.int32)[:, None],
            (token_here * shard_rows + source_row)[None, :],
            0,
        ),
        axis=1,
    )
    asked = lax.all_to_all(
        asked.reshape(n_feat, capacity), "feat", split_axis=0, concat_axis=0, tiled=True
    )
    rows = gather_rows(shard, (asked % shard_rows).reshape(-1))
    tok_dev = attention.shape[2]
    tokens_of_slot = asked // shard_rows + (
        jnp.arange(n_feat, dtype=jnp.int32) * tok_dev
    )[:, None]

    rstd_table = norm_rstd[0]
    tokens_all = rstd_table.shape[1]
    pos_table = (positions[:, None] == jnp.arange(tokens_all, dtype=jnp.int32)[None, :]).astype(
        jnp.float32
    )
    target_scale = jnp.dot(
        pos_table, rstd_table[0] * rstd_table[1], precision=lax.Precision.HIGHEST
    )
    enc_scaled = (target_enc[0].astype(jnp.float32) * gains[0] * gains[1]).astype(jnp.bfloat16)
    partial_heads = jnp.dot(enc_scaled, out_weight[0].T, preferred_element_type=jnp.float32)
    own_targets = targets // n_tgt

    def part(x, of):
        return lax.dynamic_slice_in_dim(x, of * own_targets, own_targets)

    summed_heads = part(partial_heads, me_tgt)
    for step in range(1, n_tgt):
        summed_heads = summed_heads + shifted(part(partial_heads, (me_tgt + step) % n_tgt), step)
    heads_local = (summed_heads * part(target_scale, me_tgt)[:, None]).astype(jnp.bfloat16)
    attn_local = attention[0].astype(jnp.bfloat16)
    pair = HEADS // KV * HD
    if whole_heads:
        own_kv = heads_local.shape[1] // pair
        attn_part = lax.dynamic_slice_in_dim(
            attn_local.reshape(n_tgt, -1, pair), me_tgt, 1
        )[0]
        sent = jnp.concatenate(
            [
                heads_local.reshape(own_targets, own_kv, pair).transpose(1, 0, 2).reshape(-1, pair),
                attn_part,
            ],
            axis=0,
        )
        got = lax.all_gather(sent, ("tgt", "feat"), axis=0)
        cut = own_kv * own_targets
        heads_back = got[:, :cut].reshape(n_tgt, n_feat, own_kv, own_targets, pair)
        heads_back = heads_back.transpose(1, 2, 0, 3, 4).reshape(KV, targets, pair)
        attn_all = got[:, cut:].reshape(n_tgt, n_feat, -1).transpose(1, 0, 2)
        attn_all = attn_all.reshape((n_feat,) + attn_local.shape)
        attn_all = attn_all.transpose(1, 0, 2, 3).reshape(HEADS, tokens_all, tokens_all)
    else:
        heads_back = lax.all_gather(heads_local, "feat", axis=1, tiled=True)
        heads_back = lax.all_gather(heads_back, "tgt", axis=0, tiled=True)
        heads_back = heads_back.reshape(targets, KV, pair).transpose(1, 0, 2)
        attn_all = lax.all_gather(attn_local, "feat", axis=1, tiled=True)
    chosen = jnp.einsum(
        "fq,htq->hft",
        pos_table.astype(jnp.bfloat16),
        attn_all,
        preferred_element_type=jnp.float32,
    )
    causal = jnp.arange(tokens_all, dtype=jnp.int32)[None, :] <= positions[:, None]
    picked = jnp.where(causal[None], chosen, 0.0).astype(jnp.bfloat16)

    raw = owner_scores(kv_of_block, rows, values, heads_back, picked, tokens_of_slot.reshape(1, -1))
    scores = part(raw, me_tgt).astype(jnp.float32)
    for step in range(1, n_tgt):
        scores = scores + shifted(part(raw, (me_tgt + step) % n_tgt), step).astype(jnp.float32)
    replies = lax.all_to_all(
        scores.astype(jnp.bfloat16).reshape(own_targets, n_feat, capacity).transpose(1, 0, 2),
        "feat",
        split_axis=0,
        concat_axis=0,
        tiled=True,
    )
    local_rstd = lax.dynamic_slice_in_dim(
        rstd_table[2], lax.axis_index("feat") * tok_dev, tok_dev
    )
    source_scale = jnp.repeat(local_rstd, K) * source_act * source_valid.astype(jnp.float32)
    return pl.pallas_call(
        place_kernel,
        out_shape=jax.ShapeDtypeStruct((own_targets, slot_count), jnp.bfloat16),
        compiler_params=pltpu.CompilerParams(vmem_limit_bytes=32 * 1024 * 1024),
    )(replies, flat_slot[None, :], source_scale[None, :])[None]


def solution(mesh):
    in_specs = (
        P("lay", "feat", "tgt"),
        P("lay", "feat", "tgt"),
        P("lay", "feat", "tgt"),
        P("lay", "grp", "tgt"),
        P("lay", "grp"),
        P("lay", "grp", "feat", None),
        P("lay", None, "tgt"),
        P("lay", "grp", None),
        P(("grp", "feat"), None),
        P(("grp", "feat")),
        P(("grp", "feat")),
        P(("grp", "feat")),
    )
    out_specs = P("lay", ("grp", "tgt"), "feat")
    return jax.shard_map(
        on_device, mesh=mesh, in_specs=in_specs, out_specs=out_specs, check_vma=False
    )
```

profile of v0, /device:TPU:0, one launch (start us, length us, event | category | flops | bytes accessed | tf_op | source)
XLA Modules:
  0.0 221.5 jit_solution(386296897046122400)
XLA Ops:
  6.5 0.0 copy-start
  6.5 0.0 all-gather.6.cloned.1.call-start
  6.5 1.0 slice_reduce_fusion.2
  7.5 2.0 fusion.5
  9.5 0.0 copy-done
  9.5 0.0 copy-start.4
  9.5 0.0 copy-start.8
  9.5 0.0 copy-start.9
  9.5 2.1 fusion
  11.6 0.0 copy-start.3
  11.7 0.0 copy-start.5
  11.7 3.0 %collective-permute-start = (f32[128,512]{1,0:T(8,128)S(1)}, f32[128,512]{1,0:T(8,128)S(1)}, u32[]{:S(2)}, u32[]{:S(2)}) collective-permute-start(f32[128,512]{1,0:T(8,128)S(1)} %constant_dynamic-slice_fusion.1), channel_id=1, source_target_pairs={{0,2},{2,0},{1,3},{3,1},{4,6},{6,4},{5,7},{7,5},{8,10},{10,8},{9,1... | collective-permute-start | bytes 786440 | tf_op jit(solution)/shard_map/ppermute | solution.py:169
  14.7 0.0 copy-done.4
  14.7 0.1 convert_element_type.64
  14.8 0.0 copy-done.8
  14.8 0.0 copy-done.9
  14.8 0.1 fusion.10
  14.9 0.1 dynamic_slice.29
  15.0 6.0 %collective-permute-done = f32[128,512]{1,0:T(8,128)S(1)} collective-permute-done((f32[128,512]{1,0:T(8,128)S(1)}, f32[128,512]{1,0:T(8,128)S(1)}, u32[]{:S(2)}, u32[]{:S(2)}) %collective-permute-start) | collective-permute-done | bytes 262176 | tf_op jit(solution)/shard_map/ppermute | solution.py:169
  21.0 0.1 multiply_convert_fusion.1
  21.1 0.7 pad_maximum_fusion
  21.8 0.0 all-gather.6.cloned.1.call-update
  21.8 0.0 all-gather.4.cloned.1.call-start
  21.9 0.7 all-gather.4.cloned.1.call-update
  22.6 0.0 copy-done.3
  22.6 1.1 reduce-window.6
  23.7 0.2 slice_reduce_fusion
  24.0 0.2 reduce-window.9
  24.1 0.1 add_bitcast_fusion
  24.2 0.0 copy-done.5
  24.3 1.5 select_reduce_fusion
  25.8 5.1 %all-to-all-start = ((s32[4,1,512]{2,1,0:T(1,128)}), s32[4,1,512]{2,1,0:T(1,128)S(1)}, u32[]{:S(2)}, u32[]{:S(2)}) async-start(s32[4,1,512]{2,1,0:T(1,128)} %bitcast.3), calls=%async_computation | async-start | bytes 16384 | tf_op jit(solution)/shard_map/all_to_all | solution.py:196
  30.9 0.1 broadcast_bitcast_fusion
  31.0 0.1 copy.33
  31.1 5.4 %all-to-all-done = s32[4,1,512]{2,1,0:T(1,128)S(1)} async-done(((s32[4,1,512]{2,1,0:T(1,128)}), s32[4,1,512]{2,1,0:T(1,128)S(1)}, u32[]{:S(2)}, u32[]{:S(2)}) %all-to-all-start) | async-done | bytes 8224 | tf_op jit(solution)/shard_map/all_to_all | solution.py:196
  36.5 117.4 %shard_map.118.rows_ref = bf16[2048,2304]{1,0:T(8,128)(2,1)S(1)} custom-call(s32[2048]{0:T(1024)S(1)} %add_select_fusion.index_ref, bf16[1024,8,2304]{2,1,0:T(8,128)(2,1)} %bitcast.88), custom_call_target="tpu_custom_call" | custom-call | flops 75497472 | bytes 84934656 | tf_op jit(solution)/shard_map/pallas_call | solution.py:61
  154.0 0.0 copy-start.2
  154.0 3.6 %copy-done.2 = bf16[2048,2304]{1,0:T(8,128)(2,1)} copy-done((bf16[2048,2304]{1,0:T(8,128)(2,1)}, bf16[2048,2304]{1,0:T(8,128)(2,1)S(1)}, u32[]{:S(2)}) %copy-start.2) | copy-done | bytes 9437208
  157.6 0.0 all-gather.6.cloned.1.call-done
  157.7 1.3 slice.47
  159.0 0.8 slice.48
  159.7 0.1 copy.32
  159.9 0.1 reshape.218
  160.0 0.5 fusion.2.picked_ref
  160.5 0.0 all-gather.4.cloned.1.call-done.values_ref
  160.6 22.6 %shard_map.119 = bf16[256,2048]{1,0:T(8,128)(2,1)S(1)} custom-call(bf16[2048,2304]{1,0:T(8,128)(2,1)} %copy-done.2, bf16[1024,2304]{1,0:T(8,128)(2,1)} %all-gather.4.cloned.1.call-done.values_ref, bf16[8,256,256]{2,1,0:T(8,128)(2,1)S(1)} %bitcast.86, bf16[16,256,32]{2,1,0:T(8,128)(2,1)S(1)} %fusion.2.picked_ref, s32[1,2048]{1,0:T(1,128)S(1)} %fusion.19.token_ref), custom_call_target="tpu_custom_call" | custom-call | tf_op jit(solution)/shard_map/pallas_call | solution.py:113
  183.3 0.0 slice-start
  183.3 0.0 copy-start.6
  183.3 0.0 copy-start.7
  183.3 1.6 collective-permute-start.1
  184.9 9.9 %collective-permute-done.1 = bf16[128,2048]{1,0:T(8,128)(2,1)S(1)} collective-permute-done((bf16[128,2048]{1,0:T(8,128)(2,1)S(1)}, bf16[128,2048]{1,0:T(8,128)(2,1)S(1)}, u32[]{:S(2)}, u32[]{:S(2)}) %collective-permute-start.1) | collective-permute-done | bytes 524320 | tf_op jit(solution)/shard_map/ppermute | solution.py:169
  194.7 0.0 copy-start.1
  194.7 0.1 add_convert_fusion
  194.9 0.3 copy.37
  195.1 1.0 copy.38
  196.2 5.9 %all-to-all-start.1 = ((bf16[4,128,512]{2,1,0:T(8,128)(2,1)}), bf16[4,128,512]{2,1,0:T(8,128)(2,1)S(1)}, u32[]{:S(2)}, u32[]{:S(2)}) async-start(bf16[4,128,512]{2,1,0:T(8,128)(2,1)} %bitcast.27), calls=%async_computation.1 | async-start | bytes 1048576 | tf_op jit(solution)/shard_map/all_to_all | solution.py:263
  202.0 0.0 slice-done
  202.0 0.1 fusion.26
  202.1 0.0 copy-done.6
  202.1 0.0 copy-done.7
  202.1 0.1 fusion.24
  202.2 11.1 %all-to-all-done.1.replies_ref = bf16[4,128,512]{2,1,0:T(8,128)(2,1)S(1)} async-done(((bf16[4,128,512]{2,1,0:T(8,128)(2,1)}), bf16[4,128,512]{2,1,0:T(8,128)(2,1)S(1)}, u32[]{:S(2)}, u32[]{:S(2)}) %all-to-all-start.1) | async-done | bytes 524320 | tf_op jit(solution)/shard_map/all_to_all | solution.py:263
  213.3 1.4 shard_map.120
  214.7 0.0 copy-done.1
  (16 shorter events, 0.3 us)
Async XLA Ops:
  6.5 3.0 %copy-start = (bf16[1,512,2304]{2,1,0:T(8,128)(2,1)S(1)}, bf16[1,512,2304]{2,1,0:T(8,128)(2,1)}, u32[]{:S(2)}) copy-start(bf16[1,512,2304]{2,1,0:T(8,128)(2,1)} %param.14) | copy-start | bytes 7077892
  6.5 151.1 %all-gather.6.cloned.1.call-start = ((), (), s32[]{:S(2)}) async-start(), calls=%async_computation.3 | async-start | bytes 1216512 | tf_op jit(solution)/shard_map/all_gather | solution.py:238
  9.5 5.2 %copy-start.4 = (f32[1,16,8,32]{3,2,1,0:T(8,128)S(1)}, f32[1,16,8,32]{3,2,1,0:T(8,128)}, u32[]{:S(2)}) copy-start(f32[1,16,8,32]{3,2,1,0:T(8,128)} %param.17) | copy-start | bytes 49156
  9.5 5.3 %copy-start.8 = (s32[1,256]{1,0:T(1,128)S(1)}, s32[1,256]{1,0:T(1,128)}, u32[]{:S(2)}) copy-start(s32[1,256]{1,0:T(1,128)} %param.16) | copy-start | bytes 3076
  9.5 5.3 %copy-start.9 = (f32[1,3,32]{2,0,1:T(1,128)S(1)}, f32[1,3,32]{2,0,1:T(1,128)}, u32[]{:S(2)}) copy-start(f32[1,3,32]{2,0,1:T(1,128)} %param.19) | copy-start | bytes 1156
  11.6 10.9 %copy-start.3 = (s32[1024,1]{0,1:T(1,128)S(1)}, s32[1024,1]{0,1:T(1,128)}, u32[]{:S(2)}) copy-start(s32[1024,1]{0,1:T(1,128)} %param.20) | copy-start | bytes 12292
  11.7 12.6 %copy-start.5 = (s32[1024]{0:T(1024)S(1)}, s32[1024]{0:T(1024)}, u32[]{:S(2)}) copy-start(s32[1024]{0:T(1024)} %param.21) | copy-start | bytes 12292
  11.7 9.3 %collective-permute-start = (f32[128,512]{1,0:T(8,128)S(1)}, f32[128,512]{1,0:T(8,128)S(1)}, u32[]{:S(2)}, u32[]{:S(2)}) collective-permute-start(f32[128,512]{1,0:T(8,128)S(1)} %constant_dynamic-slice_fusion.1), channel_id=1, source_target_pairs={{0,2},{2,0},{1,3},{3,1},{4,6},{6,4},{5,7},{7,5},{8,10},{10,8},{9,1... | collective-permute-start | bytes 786440 | tf_op jit(solution)/shard_map/ppermute | solution.py:169
  21.8 138.7 %all-gather.4.cloned.1.call-start = ((), (), s32[]{:S(2)}) async-start(), calls=%async_computation.2 | async-start | bytes 5308416 | tf_op jit(solution)/shard_map/all_gather | solution.py:180
  25.8 10.7 %all-to-all-start = ((s32[4,1,512]{2,1,0:T(1,128)}), s32[4,1,512]{2,1,0:T(1,128)S(1)}, u32[]{:S(2)}, u32[]{:S(2)}) async-start(s32[4,1,512]{2,1,0:T(1,128)} %bitcast.3), calls=%async_computation | async-start | bytes 16384 | tf_op jit(solution)/shard_map/all_to_all | solution.py:196
  154.0 3.6 %copy-start.2 = (bf16[2048,2304]{1,0:T(8,128)(2,1)}, bf16[2048,2304]{1,0:T(8,128)(2,1)S(1)}, u32[]{:S(2)}) copy-start(bf16[2048,2304]{1,0:T(8,128)(2,1)S(1)} %shard_map.118.rows_ref) | copy-start | bytes 28311556
  183.3 18.8 %slice-start = ((f32[1,3,32]{2,0,1:T(1,128)}), f32[1,1,32]{2,0,1:T(1,128)S(1)}, s32[]{:S(2)}) async-start(f32[1,3,32]{2,0,1:T(1,128)} %param.19), calls=%async_computation.4 | async-start | bytes 1024 | tf_op jit(solution)/shard_map/slice | solution.py:271
  183.3 18.8 %copy-start.6 = (f32[1024]{0:T(1024)S(1)}, f32[1024]{0:T(1024)}, u32[]{:S(2)}) copy-start(f32[1024]{0:T(1024)} %param.22) | copy-start | bytes 12292
  183.3 18.8 %copy-start.7 = (s32[1024]{0:T(1024)S(1)}, s32[1024]{0:T(1024)}, u32[]{:S(2)}) copy-start(s32[1024]{0:T(1024)} %param.23) | copy-start | bytes 12292
  183.3 11.4 %collective-permute-start.1 = (bf16[128,2048]{1,0:T(8,128)(2,1)S(1)}, bf16[128,2048]{1,0:T(8,128)(2,1)S(1)}, u32[]{:S(2)}, u32[]{:S(2)}) collective-permute-start(bf16[128,2048]{1,0:T(8,128)(2,1)S(1)} %constant_dynamic-slice_fusion), channel_id=1, source_target_pairs={{0,2},{2,0},{1,3},{3,1},{4,6},{6,4},{5,7},{7,5},{8,10},{10,8},{9,1... | collective-permute-start | bytes 1572872 | tf_op jit(solution)/shard_map/ppermute | solution.py:169
  194.7 20.0 %copy-start.1 = (bf16[1,512,2304]{2,1,0:T(8,128)(2,1)S(1)}, bf16[1,512,2304]{2,1,0:T(8,128)(2,1)}, u32[]{:S(2)}) copy-start(bf16[1,512,2304]{2,1,0:T(8,128)(2,1)} %param.14) | copy-start | bytes 7077892
  196.2 17.1 %all-to-all-start.1 = ((bf16[4,128,512]{2,1,0:T(8,128)(2,1)}), bf16[4,128,512]{2,1,0:T(8,128)(2,1)S(1)}, u32[]{:S(2)}, u32[]{:S(2)}) async-start(bf16[4,128,512]{2,1,0:T(8,128)(2,1)} %bitcast.27), calls=%async_computation.1 | async-start | bytes 1048576 | tf_op jit(solution)/shard_map/all_to_all | solution.py:263
Sparse Core Ops, SparseCore 0:
  21.9 41.9 all-gather.5
  66.0 78.7 all-gather.3
where the time goes:
time: 225 us; the launch traced here: 222 us
  Pallas kernels  142 us (63%)
  waiting for transfers between devices  33 us (15%)
  starting transfers between devices  15.6 us (7%)
  between operations  13.7 us (6%)
  local copies, waits for them, and re-layouts  8.99 us (4%)
  other arithmetic  5.99 us (3%)
  matrix products  2.72 us (1%)
    pallas_call x1, Pallas kernels, gather_rows(): pl.pallas_call(gather_kernel, grid_spec=pltpu.PrefetchScalarGridSpec(num_...  117 us
    pallas_call x1, Pallas kernels, owner_scores(): pl.pallas_call(functools.partial(score_kernel, kv_of_block), grid=(slots...  22.6 us
    ppermute x2, waiting for transfers between devices, shifted(): lax.ppermute(x, 'tgt', [(i, (i + step) % n_tgt) for i in range(n_tgt)])  15.8 us
    all_to_all x1, waiting for transfers between devices, on_device(): lax.all_to_all(scores.astype(jnp.bfloat16).reshape(own_targets, n_feat, c...  11.1 us
    all_to_all x1, starting transfers between devices, on_device(): lax.all_to_all(scores.astype(jnp.bfloat16).reshape(own_targets, n_feat, c...  5.86 us
    all_to_all x1, waiting for transfers between devices, on_device(): lax.all_to_all(asked.reshape(n_feat, capacity), 'feat', split_axis=0, con...  5.36 us
    all_to_all x1, starting transfers between devices, on_device(): lax.all_to_all(asked.reshape(n_feat, capacity), 'feat', split_axis=0, con...  5.12 us
    ppermute x2, starting transfers between devices, shifted(): lax.ppermute(x, 'tgt', [(i, (i + step) % n_tgt) for i in range(n_tgt)])  4.57 us
  transfers between devices with their start and end apart: 6, of which 4 were waited for; matrix products, arithmetic and copies ran while one was open for 3% of the time, Pallas kernels for 53%

commit v1 on v0

--- a/solution.py
+++ b/solution.py
@@ -188,7 +188,7 @@
     asked = jnp.sum(
         jnp.where(
             flat_slot[None, :] == jnp.arange(n_feat * capacity, dtype=jnp.int32)[:, None],
-            (token_here * shard_rows + source_row)[None, :],
+            (token_here * shard_rows + source_row + 1)[None, :],
             0,
         ),
         axis=1,
@@ -196,6 +196,8 @@
     asked = lax.all_to_all(
         asked.reshape(n_feat, capacity), "feat", split_axis=0, concat_axis=0, tiled=True
     )
+    spare = jnp.arange(n_feat * capacity, dtype=jnp.int32).reshape(n_feat, capacity)
+    asked = jnp.where(asked > 0, asked - 1, spare * 8 % shard_rows)
     rows = gather_rows(shard, (asked % shard_rows).reshape(-1))
     tok_dev = attention.shape[2]
     tokens_of_slot = asked // shard_rows + (
@@ -235,7 +237,13 @@
             ],
             axis=0,
         )
-        got = lax.all_gather(sent, ("tgt", "feat"), axis=0)
+        got = lax.all_to_all(
+            jnp.broadcast_to(sent[None], (n_tgt * n_feat,) + sent.shape),
+            ("tgt", "feat"),
+            split_axis=0,
+            concat_axis=0,
+            tiled=True,
+        )
         cut = own_kv * own_targets
         heads_back = got[:, :cut].reshape(n_tgt, n_feat, own_kv, own_targets, pair)
         heads_back = heads_back.transpose(1, 2, 0, 3, 4).reshape(KV, targets, pair)

time: 225 us -> 174 us (0.77)
  Pallas kernels: 142 us -> 61.1 us
  waiting for transfers between devices: 33 us -> 63.2 us
    pallas_call x1, Pallas kernels: 117 us -> 37 us  [gather_rows(): pl.pallas_call(gather_kernel, grid_spec=pltpu.PrefetchScalarGridSpec(num_...]
    all_gather x1, waiting for transfers between devices: 0.02 us -> 33.2 us  [on_device(): values = lax.all_gather(half, ('grp', 'feat'), axis=0, tiled=True)]
    ppermute x2, waiting for transfers between devices: 15.8 us -> 11.2 us  [shifted(): lax.ppermute(x, 'tgt', [(i, (i + step) % n_tgt) for i in range(n_tgt)])]
    all_to_all x0 -> x1, starting transfers between devices: none -> 3.56 us  [on_device(): lax.all_to_all(jnp.broadcast_to(sent[None], (n_tgt * n_feat,) + sent.shap...]
    all_to_all x1, waiting for transfers between devices: 11.1 us -> 13.7 us  [on_device(): lax.all_to_all(scores.astype(jnp.bfloat16).reshape(own_targets, n_feat, c...]
  transfers between devices with their start and end apart: 6 -> 6, of which waited for: 4 -> 4; matrix products, arithmetic and copies ran while one was open for 3% -> 5% of each run, Pallas kernels for 53% -> 22%
where the time goes in v1:
time: 174 us; the launch traced here: 171 us
  waiting for transfers between devices  63.2 us (36%)
  Pallas kernels  61.1 us (35%)
  starting transfers between devices  16.9 us (10%)
  between operations  13.8 us (8%)
  local copies, waits for them, and re-layouts  8.07 us (5%)
  other arithmetic  5.47 us (3%)
  matrix products  2.71 us (2%)
    pallas_call x1, Pallas kernels, gather_rows(): pl.pallas_call(gather_kernel, grid_spec=pltpu.PrefetchScalarGridSpec(num_...  37 us
    all_gather x1, waiting for transfers between devices, on_device(): values = lax.all_gather(half, ('grp', 'feat'), axis=0, tiled=True)  33.2 us
    pallas_call x1, Pallas kernels, owner_scores(): pl.pallas_call(functools.partial(score_kernel, kv_of_block), grid=(slots...  22.6 us
    all_to_all x1, waiting for transfers between devices, on_device(): lax.all_to_all(scores.astype(jnp.bfloat16).reshape(own_targets, n_feat, c...  13.7 us
    ppermute x2, waiting for transfers between devices, shifted(): lax.ppermute(x, 'tgt', [(i, (i + step) % n_tgt) for i in range(n_tgt)])  11.2 us
    all_to_all x1, waiting for transfers between devices, on_device(): lax.all_to_all(asked.reshape(n_feat, capacity), 'feat', split_axis=0, con...  5.16 us
    all_to_all x1, starting transfers between devices, on_device(): lax.all_to_all(asked.reshape(n_feat, capacity), 'feat', split_axis=0, con...  4.87 us
    ppermute x2, starting transfers between devices, shifted(): lax.ppermute(x, 'tgt', [(i, (i + step) % n_tgt) for i in range(n_tgt)])  4.55 us
  transfers between devices with their start and end apart: 6, of which 4 were waited for; matrix products, arithmetic and copies ran while one was open for 5% of the time, Pallas kernels for 22%

profile of v1, /device:TPU:0, one launch (start us, length us, event | category | flops | bytes accessed | tf_op | source)
XLA Modules:
  0.0 171.2 jit_solution(8614321540678176108)
XLA Ops:
  6.5 0.0 copy-start
  6.5 0.0 all-gather.2.cloned.1.call-start
  6.5 1.0 slice_reduce_fusion.2
  7.5 2.0 %fusion.5 = bf16[128,2304]{1,0:T(8,128)(2,1)} fusion(f32[2304]{0:T(1024)S(1)} %get-tuple-element.10, bf16[256,2304]{1,0:T(8,128)(2,1)} %bitcast.102, s32[]{:T(128)S(6)} %select_n.91), kind=kLoop, calls=%fused_computation.9 | loop fusion | flops 884736 | bytes 1188868 | tf_op jit(solution)/shard_map/convert_element_type | solution.py:171
  9.5 0.0 all-gather.2.cloned.1.call-update
  9.6 0.0 copy-done
  9.6 0.0 copy-start.3
  9.6 0.0 copy-start.5
  9.6 0.0 copy-start.4
  9.6 0.0 copy-start.8
  9.6 0.0 copy-start.9
  9.6 2.1 %fusion = f32[256,512]{1,0:T(8,128)S(1)} fusion(bf16[1,512,2304]{2,1,0:T(8,128)(2,1)S(1)} %copy-done, bf16[1,256,2304]{2,1,0:T(8,128)(2,1)} %param.15, f32[2304]{0:T(1024)S(1)} %get-tuple-element.11, f32[2304]{0:T(1024)S(1)} %get-tuple-element.9), kind=kOutput, calls=%fused_computation.2 | convolution fusion | flops 606339072 | bytes 4081664 | tf_op jit(solution)/shard_map/dot_general | solution.py:216
  11.8 3.0 %collective-permute-start = (f32[128,512]{1,0:T(8,128)S(1)}, f32[128,512]{1,0:T(8,128)S(1)}, u32[]{:S(2)}, u32[]{:S(2)}) collective-permute-start(f32[128,512]{1,0:T(8,128)S(1)} %constant_dynamic-slice_fusion.1), channel_id=1, source_target_pairs={{0,2},{2,0},{1,3},{3,1},{4,6},{6,4},{5,7},{7,5},{8,10},{10,8},{9,1... | collective-permute-start | bytes 786440 | tf_op jit(solution)/shard_map/ppermute | solution.py:169
  14.8 0.0 copy-done.3
  14.8 1.1 reduce-window.6
  15.9 0.2 slice_reduce_fusion
  16.1 0.2 reduce-window.9
  16.3 0.1 add_bitcast_fusion
  16.4 0.0 copy-done.5
  16.5 1.5 select_reduce_fusion
  18.0 4.9 %all-to-all-start = ((s32[4,1,512]{2,1,0:T(1,128)}), s32[4,1,512]{2,1,0:T(1,128)S(1)}, u32[]{:S(2)}, u32[]{:S(2)}) async-start(s32[4,1,512]{2,1,0:T(1,128)} %bitcast.3), calls=%async_computation | async-start | bytes 16384 | tf_op jit(solution)/shard_map/all_to_all | solution.py:196
  22.9 0.0 copy-done.4
  22.9 0.1 convert_element_type.64
  23.0 0.0 copy-done.8
  23.0 0.0 copy-done.9
  23.0 0.1 fusion.10
  23.1 0.1 dynamic_slice.29
  23.2 0.0 collective-permute-done
  23.2 0.1 multiply_convert_fusion.1
  23.3 5.2 %all-to-all-done = s32[4,1,512]{2,1,0:T(1,128)S(1)} async-done(((s32[4,1,512]{2,1,0:T(1,128)}), s32[4,1,512]{2,1,0:T(1,128)S(1)}, u32[]{:S(2)}, u32[]{:S(2)}) %all-to-all-start) | async-done | bytes 8224 | tf_op jit(solution)/shard_map/all_to_all | solution.py:196
  28.5 1.1 broadcast_in_dim.51
  29.5 3.6 %all-to-all-start.1 = ((bf16[8,264,256]{2,1,0:T(8,128)(2,1)}), bf16[8,264,256]{2,1,0:T(8,128)(2,1)S(1)}, u32[]{:S(2)}, u32[]{:S(2)}) async-start(bf16[8,264,256]{2,1,0:T(8,128)(2,1)} %broadcast_in_dim.51), calls=%async_computation.1 | async-start | bytes 2162688 | tf_op jit(solution)/shard_map/all_to_all | solution.py:240
  33.1 0.1 copy.41
  33.3 0.1 broadcast_bitcast_fusion
  33.5 37.0 %shard_map.118.rows_ref = bf16[2048,2304]{1,0:T(8,128)(2,1)S(1)} custom-call(s32[2048]{0:T(1024)S(1)} %add_select_fusion.index_ref, bf16[1024,8,2304]{2,1,0:T(8,128)(2,1)} %bitcast.97), custom_call_target="tpu_custom_call" | custom-call | flops 75497472 | bytes 84934656 | tf_op jit(solution)/shard_map/pallas_call | solution.py:61
  70.5 0.0 copy-start.2
  70.6 3.6 %copy-done.2 = bf16[2048,2304]{1,0:T(8,128)(2,1)} copy-done((bf16[2048,2304]{1,0:T(8,128)(2,1)}, bf16[2048,2304]{1,0:T(8,128)(2,1)S(1)}, u32[]{:S(2)}) %copy-start.2) | copy-done | bytes 9437208
  74.2 0.1 fusion.23.token_ref
  74.3 0.0 all-to-all-done.1
  74.3 0.1 slice.47
  74.3 0.1 copy.40
  74.5 0.1 reshape.310
  74.6 0.5 fusion.2.picked_ref
  75.1 33.2 %all-gather.2.cloned.1.call-done.values_ref = bf16[1024,2304]{1,0:T(8,128)(2,1)} async-done(((bf16[128,2304]{1,0:T(8,128)(2,1)}), bf16[1024,2304]{1,0:T(8,128)(2,1)}) %all-gather.2.cloned.1.call-update) | async-done | bytes 4718608 | tf_op jit(solution)/shard_map/all_gather | solution.py:180
  108.3 22.6 %shard_map.119 = bf16[256,2048]{1,0:T(8,128)(2,1)S(1)} custom-call(bf16[2048,2304]{1,0:T(8,128)(2,1)} %copy-done.2, bf16[1024,2304]{1,0:T(8,128)(2,1)} %all-gather.2.cloned.1.call-done.values_ref, bf16[8,256,256]{2,1,0:T(8,128)(2,1)S(1)} %bitcast.95, bf16[16,256,32]{2,1,0:T(8,128)(2,1)S(1)} %fusion.2.picked_ref, s32[1,2048]{1,0:T(1,128)S(1)} %fusion.23.token_ref), custom_call_target="tpu_custom_call" | custom-call | tf_op jit(solution)/shard_map/pallas_call | solution.py:113
  131.0 0.0 slice-start
  131.0 0.0 copy-start.6
  131.0 0.0 copy-start.7
  131.0 1.5 collective-permute-start.1
  132.6 11.2 %collective-permute-done.1 = bf16[128,2048]{1,0:T(8,128)(2,1)S(1)} collective-permute-done((bf16[128,2048]{1,0:T(8,128)(2,1)S(1)}, bf16[128,2048]{1,0:T(8,128)(2,1)S(1)}, u32[]{:S(2)}, u32[]{:S(2)}) %collective-permute-start.1) | collective-permute-done | bytes 524320 | tf_op jit(solution)/shard_map/ppermute | solution.py:169
  143.7 0.0 copy-start.1
  143.7 0.1 add_convert_fusion
  143.9 0.3 copy.45
  144.1 1.0 copy.46
  145.1 3.9 %all-to-all-start.2 = ((bf16[4,128,512]{2,1,0:T(8,128)(2,1)}), bf16[4,128,512]{2,1,0:T(8,128)(2,1)S(1)}, u32[]{:S(2)}, u32[]{:S(2)}) async-start(bf16[4,128,512]{2,1,0:T(8,128)(2,1)} %bitcast.27), calls=%async_computation.2 | async-start | bytes 1048576 | tf_op jit(solution)/shard_map/all_to_all | solution.py:271
  149.1 0.0 slice-done
  149.1 0.1 fusion.33
  149.1 0.0 copy-done.6
  149.1 0.0 copy-done.7
  149.2 0.1 fusion.31
  149.2 13.7 %all-to-all-done.2.replies_ref = bf16[4,128,512]{2,1,0:T(8,128)(2,1)S(1)} async-done(((bf16[4,128,512]{2,1,0:T(8,128)(2,1)}), bf16[4,128,512]{2,1,0:T(8,128)(2,1)S(1)}, u32[]{:S(2)}, u32[]{:S(2)}) %all-to-all-start.2) | async-done | bytes 524320 | tf_op jit(solution)/shard_map/all_to_all | solution.py:271
  162.9 1.4 shard_map.120
  164.3 0.0 copy-done.1
  (24 shorter events, 0.3 us)
Async XLA Ops:
  6.5 3.0 %copy-start = (bf16[1,512,2304]{2,1,0:T(8,128)(2,1)S(1)}, bf16[1,512,2304]{2,1,0:T(8,128)(2,1)}, u32[]{:S(2)}) copy-start(bf16[1,512,2304]{2,1,0:T(8,128)(2,1)} %param.14) | copy-start | bytes 7077892
  6.5 101.8 %all-gather.2.cloned.1.call-start = ((), (), s32[]{:S(2)}) async-start(), calls=%async_computation.3 | async-start | bytes 5308416 | tf_op jit(solution)/shard_map/all_gather | solution.py:180
  9.6 5.2 %copy-start.3 = (s32[1024,1]{0,1:T(1,128)S(1)}, s32[1024,1]{0,1:T(1,128)}, u32[]{:S(2)}) copy-start(s32[1024,1]{0,1:T(1,128)} %param.20) | copy-start | bytes 12292
  9.6 6.9 %copy-start.5 = (s32[1024]{0:T(1024)S(1)}, s32[1024]{0:T(1024)}, u32[]{:S(2)}) copy-start(s32[1024]{0:T(1024)} %param.21) | copy-start | bytes 12292
  9.6 13.3 %copy-start.4 = (f32[1,16,8,32]{3,2,1,0:T(8,128)S(1)}, f32[1,16,8,32]{3,2,1,0:T(8,128)}, u32[]{:S(2)}) copy-start(f32[1,16,8,32]{3,2,1,0:T(8,128)} %param.17) | copy-start | bytes 49156
  9.6 13.4 %copy-start.8 = (s32[1,256]{1,0:T(1,128)S(1)}, s32[1,256]{1,0:T(1,128)}, u32[]{:S(2)}) copy-start(s32[1,256]{1,0:T(1,128)} %param.16) | copy-start | bytes 3076
  9.6 13.3 %copy-start.9 = (f32[1,3,32]{2,0,1:T(1,128)S(1)}, f32[1,3,32]{2,0,1:T(1,128)}, u32[]{:S(2)}) copy-start(f32[1,3,32]{2,0,1:T(1,128)} %param.19) | copy-start | bytes 1156
  11.8 11.4 %collective-permute-start = (f32[128,512]{1,0:T(8,128)S(1)}, f32[128,512]{1,0:T(8,128)S(1)}, u32[]{:S(2)}, u32[]{:S(2)}) collective-permute-start(f32[128,512]{1,0:T(8,128)S(1)} %constant_dynamic-slice_fusion.1), channel_id=1, source_target_pairs={{0,2},{2,0},{1,3},{3,1},{4,6},{6,4},{5,7},{7,5},{8,10},{10,8},{9,1... | collective-permute-start | bytes 786440 | tf_op jit(solution)/shard_map/ppermute | solution.py:169
  18.0 10.5 %all-to-all-start = ((s32[4,1,512]{2,1,0:T(1,128)}), s32[4,1,512]{2,1,0:T(1,128)S(1)}, u32[]{:S(2)}, u32[]{:S(2)}) async-start(s32[4,1,512]{2,1,0:T(1,128)} %bitcast.3), calls=%async_computation | async-start | bytes 16384 | tf_op jit(solution)/shard_map/all_to_all | solution.py:196
  29.5 44.7 %all-to-all-start.1 = ((bf16[8,264,256]{2,1,0:T(8,128)(2,1)}), bf16[8,264,256]{2,1,0:T(8,128)(2,1)S(1)}, u32[]{:S(2)}, u32[]{:S(2)}) async-start(bf16[8,264,256]{2,1,0:T(8,128)(2,1)} %broadcast_in_dim.51), calls=%async_computation.1 | async-start | bytes 2162688 | tf_op jit(solution)/shard_map/all_to_all | solution.py:240
  70.5 3.6 %copy-start.2 = (bf16[2048,2304]{1,0:T(8,128)(2,1)}, bf16[2048,2304]{1,0:T(8,128)(2,1)S(1)}, u32[]{:S(2)}) copy-start(bf16[2048,2304]{1,0:T(8,128)(2,1)S(1)} %shard_map.118.rows_ref) | copy-start | bytes 28311556
  131.0 18.1 %slice-start = ((f32[1,3,32]{2,0,1:T(1,128)}), f32[1,1,32]{2,0,1:T(1,128)S(1)}, s32[]{:S(2)}) async-start(f32[1,3,32]{2,0,1:T(1,128)} %param.19), calls=%async_computation.4 | async-start | bytes 1024 | tf_op jit(solution)/shard_map/slice | solution.py:279
  131.0 18.2 %copy-start.6 = (f32[1024]{0:T(1024)S(1)}, f32[1024]{0:T(1024)}, u32[]{:S(2)}) copy-start(f32[1024]{0:T(1024)} %param.22) | copy-start | bytes 12292
  131.0 18.1 %copy-start.7 = (s32[1024]{0:T(1024)S(1)}, s32[1024]{0:T(1024)}, u32[]{:S(2)}) copy-start(s32[1024]{0:T(1024)} %param.23) | copy-start | bytes 12292
  131.0 12.7 %collective-permute-start.1 = (bf16[128,2048]{1,0:T(8,128)(2,1)S(1)}, bf16[128,2048]{1,0:T(8,128)(2,1)S(1)}, u32[]{:S(2)}, u32[]{:S(2)}) collective-permute-start(bf16[128,2048]{1,0:T(8,128)(2,1)S(1)} %constant_dynamic-slice_fusion), channel_id=1, source_target_pairs={{0,2},{2,0},{1,3},{3,1},{4,6},{6,4},{5,7},{7,5},{8,10},{10,8},{9,1... | collective-permute-start | bytes 1572872 | tf_op jit(solution)/shard_map/ppermute | solution.py:169
  143.7 20.6 %copy-start.1 = (bf16[1,512,2304]{2,1,0:T(8,128)(2,1)S(1)}, bf16[1,512,2304]{2,1,0:T(8,128)(2,1)}, u32[]{:S(2)}) copy-start(bf16[1,512,2304]{2,1,0:T(8,128)(2,1)} %param.14) | copy-start | bytes 7077892
  145.1 17.7 %all-to-all-start.2 = ((bf16[4,128,512]{2,1,0:T(8,128)(2,1)}), bf16[4,128,512]{2,1,0:T(8,128)(2,1)S(1)}, u32[]{:S(2)}, u32[]{:S(2)}) async-start(bf16[4,128,512]{2,1,0:T(8,128)(2,1)} %bitcast.27), calls=%async_computation.2 | async-start | bytes 1048576 | tf_op jit(solution)/shard_map/all_to_all | solution.py:271
Sparse Core Ops, SparseCore 0:
  9.7 98.5 all-gather.1

commit v2 on v1

--- a/solution.py
+++ b/solution.py
@@ -78,7 +78,8 @@
     )(index, shard.reshape(shard.shape[0] // 8, 8, width))
 
 
-def score_kernel(kv_of_block, rows_ref, values_ref, heads_ref, picked_ref, token_ref, out_ref):
+def score_kernel(kv_of_block, rows_ref, values_ref, heads_ref, picked_ref, token_ref, *more):
+    out_ref = more[-1]
     group = HEADS // KV
     projected = lax.dot_general(
         values_ref[...],
@@ -90,8 +91,8 @@
     slots = token_ref.shape[1]
     which = lax.broadcasted_iota(jnp.int32, (tokens, slots), 0) == token_ref[...]
     which = jnp.where(which, 1.0, 0.0).astype(jnp.bfloat16)
-    total = jnp.zeros(out_ref.shape, jnp.float32)
-    for block in range(KV):
+    total = more[0][...] if len(more) == 2 else jnp.zeros(out_ref.shape, jnp.float32)
+    for block in range(len(kv_of_block)):
         kv = kv_of_block[block]
         for g in range(group):
             match = jnp.dot(
@@ -103,10 +104,10 @@
                 picked_ref[kv * group + g], which, preferred_element_type=jnp.float32
             )
             total = total + match * weight
-    out_ref[...] = total.astype(jnp.bfloat16)
-
-
-def owner_scores(kv_of_block, rows, values, heads, picked, tokens_of_slot):
+    out_ref[...] = total.astype(out_ref.dtype)
+
+
+def owner_scores(kv_of_block, rows, values, heads, picked, tokens_of_slot, dtype, base=()):
     slots, width = rows.shape
     targets = heads.shape[1]
     block = 512
@@ -119,11 +120,17 @@
             pl.BlockSpec(heads.shape, lambda i: (0, 0, 0)),
             pl.BlockSpec(picked.shape, lambda i: (0, 0, 0)),
             pl.BlockSpec((1, block), lambda i: (0, i)),
-        ],
+        ]
+        + [pl.BlockSpec((targets, block), lambda i: (0, i))] * len(base),
         out_specs=pl.BlockSpec((targets, block), lambda i: (0, i)),
-        out_shape=jax.ShapeDtypeStruct((targets, slots), jnp.bfloat16),
+        out_shape=jax.ShapeDtypeStruct((targets, slots), dtype),
         compiler_params=pltpu.CompilerParams(vmem_limit_bytes=48 * 1024 * 1024),
-    )(rows, values, heads, picked, tokens_of_slot)
+        cost_estimate=pl.CostEstimate(
+            flops=2 * slots * values.shape[0] * (width + 4 * targets),
+            bytes_accessed=2 * slots * width,
+            transcendentals=0,
+        ),
+    )(rows, values, heads, picked, tokens_of_slot, *base)
 
 
 def place_kernel(replies_ref, place_ref, scale_ref, out_ref):
@@ -170,16 +177,16 @@
 
     gained_values = (value_weight[0].astype(jnp.float32) * gains[2]).astype(jnp.bfloat16)
     n_grp = lax.axis_size("grp")
-    me_grp = lax.axis_index("grp")
-    kv_of_block = list(range(KV))
+    kv_of_block = [list(range(KV))]
     whole_heads = gained_values.shape[0] == n_grp * HD and n_grp == 2
     if whole_heads:
-        half = lax.dynamic_slice_in_dim(gained_values, me_grp * HD, HD)
-        target_enc, half = lax.optimization_barrier((target_enc, half))
-        kv_of_block = [n_grp * j + g for g in range(n_grp) for j in range(n_feat)]
-        values = lax.all_gather(half, ("grp", "feat"), axis=0, tiled=True)
+        values = [
+            lax.all_gather(gained_values[g * HD : (g + 1) * HD], "feat", axis=0, tiled=True)
+            for g in range(2)
+        ]
+        kv_of_block = [[2 * j + g for j in range(n_feat)] for g in range(2)]
     else:
-        values = lax.all_gather(gained_values, "feat", axis=0, tiled=True)
+        values = [lax.all_gather(gained_values, "feat", axis=0, tiled=True)]
 
     member = (owners[:, None] == jnp.arange(n_feat, dtype=jnp.int32)[None, :]).astype(jnp.int32)
     ranks = jnp.sum((jnp.cumsum(member, axis=0) - 1) * member, axis=1)
@@ -264,7 +271,20 @@
     causal = jnp.arange(tokens_all, dtype=jnp.int32)[None, :] <= positions[:, None]
     picked = jnp.where(causal[None], chosen, 0.0).astype(jnp.bfloat16)
 
-    raw = owner_scores(kv_of_block, rows, values, heads_back, picked, tokens_of_slot.reshape(1, -1))
+    base = ()
+    for i in range(len(values)):
+        dtype = jnp.bfloat16 if i == len(values) - 1 else jnp.float32
+        raw = owner_scores(
+            kv_of_block[i],
+            rows,
+            values[i],
+            heads_back,
+            picked,
+            tokens_of_slot.reshape(1, -1),
+            dtype,
+            base,
+        )
+        base = (raw,)
     scores = part(raw, me_tgt).astype(jnp.float32)
     for step in range(1, n_tgt):
         scores = scores + shifted(part(raw, (me_tgt + step) % n_tgt), step).astype(jnp.float32)

time: 174 us -> 196 us (1.13)
  waiting for transfers between devices: 63.2 us -> 78.5 us
  local copies, waits for them, and re-layouts: 8.07 us -> 12.2 us
  Pallas kernels: 61.1 us -> 63.6 us
    all_to_all x1, waiting for transfers between devices: 0.01 us -> 11.5 us  [on_device(): lax.all_to_all(jnp.broadcast_to(sent[None], (n_tgt * n_feat,) + sent.shap...]
    unnamed x25 -> x29, local copies, waits for them, and re-layouts: 3.77 us -> 6.8 us
    pallas_call x1 -> x2, Pallas kernels: 22.6 us -> 25.6 us  [owner_scores(): pl.pallas_call(functools.partial(score_kernel, kv_of_block), grid=(slots...]
    all_gather x1 -> x2, waiting for transfers between devices: 33.2 us -> 36 us  [on_device(): lax.all_gather(gained_values[g * HD:(g + 1) * HD], 'feat', axis=0, tiled=...]
  transfers between devices with their start and end apart: 6 -> 7, of which waited for: 4 -> 5; matrix products, arithmetic and copies ran while one was open for 5% -> 4% of each run, Pallas kernels for 22% -> 26%
where the time goes in v2:
time: 196 us; the launch traced here: 192 us
  waiting for transfers between devices  78.5 us (40%)
  Pallas kernels  63.6 us (32%)
  starting transfers between devices  16.5 us (8%)
  between operations  13.8 us (7%)
  local copies, waits for them, and re-layouts  12.2 us (6%)
  other arithmetic  4.92 us (3%)
  matrix products  2.71 us (1%)
    pallas_call x1, Pallas kernels, gather_rows(): pl.pallas_call(gather_kernel, grid_spec=pltpu.PrefetchScalarGridSpec(num_...  36.6 us
    all_gather x2, waiting for transfers between devices, on_device(): lax.all_gather(gained_values[g * HD:(g + 1) * HD], 'feat', axis=0, tiled=...  36 us
    pallas_call x2, Pallas kernels, owner_scores(): pl.pallas_call(functools.partial(score_kernel, kv_of_block), grid=(slots...  25.6 us
    all_to_all x1, waiting for transfers between devices, on_device(): lax.all_to_all(scores.astype(jnp.bfloat16).reshape(own_targets, n_feat, c...  13.6 us
    ppermute x2, waiting for transfers between devices, shifted(): lax.ppermute(x, 'tgt', [(i, (i + step) % n_tgt) for i in range(n_tgt)])  12.2 us
    all_to_all x1, waiting for transfers between devices, on_device(): lax.all_to_all(jnp.broadcast_to(sent[None], (n_tgt * n_feat,) + sent.shap...  11.5 us
    unnamed x29, local copies, waits for them, and re-layouts  6.8 us
    all_to_all x1, waiting for transfers between devices, on_device(): lax.all_to_all(asked.reshape(n_feat, capacity), 'feat', split_axis=0, con...  5.24 us
  transfers between devices with their start and end apart: 7, of which 5 were waited for; matrix products, arithmetic and copies ran while one was open for 4% of the time, Pallas kernels for 26%

profile of v2, /device:TPU:0, one launch (start us, length us, event | category | flops | bytes accessed | tf_op | source)
XLA Modules:
  0.0 192.3 jit_solution(15335259358609264693)
XLA Ops:
  6.5 0.0 copy-start
  6.5 0.0 all-gather.5.cloned.1.call-start
  6.5 1.0 slice_reduce_fusion.2
  7.5 1.5 fusion
  9.0 1.1 fusion.37
  10.1 0.0 all-gather.5.cloned.1.call-update
  10.1 0.0 all-gather.3.cloned.1.call-start
  10.2 0.0 copy-done
  10.2 0.0 copy-start.5
  10.2 0.0 copy-start.7
  10.2 0.0 copy-start.6
  10.2 0.0 copy-start.10
  10.2 0.0 copy-start.11
  10.2 2.1 %fusion.1 = f32[256,512]{1,0:T(8,128)S(1)} fusion(bf16[1,512,2304]{2,1,0:T(8,128)(2,1)S(1)} %copy-done, bf16[1,256,2304]{2,1,0:T(8,128)(2,1)} %param.15, f32[2304]{0:T(1024)S(1)} %get-tuple-element.7, f32[2304]{0:T(1024)S(1)} %get-tuple-element.5), kind=kOutput, calls=%fused_computation.4 | convolution fusion | flops 606339072 | bytes 4081664 | tf_op jit(solution)/shard_map/dot_general | solution.py:223
  12.4 3.0 %collective-permute-start = (f32[128,512]{1,0:T(8,128)S(1)}, f32[128,512]{1,0:T(8,128)S(1)}, u32[]{:S(2)}, u32[]{:S(2)}) collective-permute-start(f32[128,512]{1,0:T(8,128)S(1)} %constant_dynamic-slice_fusion.1), channel_id=1, source_target_pairs={{0,2},{2,0},{1,3},{3,1},{4,6},{6,4},{5,7},{7,5},{8,10},{10,8},{9,1... | collective-permute-start | bytes 786440 | tf_op jit(solution)/shard_map/ppermute | solution.py:176
  15.4 0.0 all-gather.3.cloned.1.call-update
  15.4 0.0 copy-done.5
  15.4 1.1 reduce-window.6
  16.6 0.2 slice_reduce_fusion
  16.8 0.2 reduce-window.9
  17.0 0.1 add_bitcast_fusion
  17.1 0.0 copy-done.7
  17.1 1.5 select_reduce_fusion
  18.6 4.9 %all-to-all-start = ((s32[4,1,512]{2,1,0:T(1,128)}), s32[4,1,512]{2,1,0:T(1,128)S(1)}, u32[]{:S(2)}, u32[]{:S(2)}) async-start(s32[4,1,512]{2,1,0:T(1,128)} %bitcast.3), calls=%async_computation | async-start | bytes 16384 | tf_op jit(solution)/shard_map/all_to_all | solution.py:203
  23.5 0.0 copy-done.6
  23.5 0.1 convert_element_type.64
  23.6 0.1 fusion.10
  23.7 0.1 dynamic_slice.25
  23.8 0.0 collective-permute-done
  23.8 0.1 multiply_convert_fusion.1
  24.0 5.2 %all-to-all-done = s32[4,1,512]{2,1,0:T(1,128)S(1)} async-done(((s32[4,1,512]{2,1,0:T(1,128)}), s32[4,1,512]{2,1,0:T(1,128)S(1)}, u32[]{:S(2)}, u32[]{:S(2)}) %all-to-all-start) | async-done | bytes 8224 | tf_op jit(solution)/shard_map/all_to_all | solution.py:203
  29.2 1.1 broadcast_in_dim.51
  30.3 3.6 %all-to-all-start.1 = ((bf16[8,264,256]{2,1,0:T(8,128)(2,1)}), bf16[8,264,256]{2,1,0:T(8,128)(2,1)S(1)}, u32[]{:S(2)}, u32[]{:S(2)}) async-start(bf16[8,264,256]{2,1,0:T(8,128)(2,1)} %broadcast_in_dim.51), calls=%async_computation.1 | async-start | bytes 2162688 | tf_op jit(solution)/shard_map/all_to_all | solution.py:247
  33.9 0.1 copy.41
  34.0 0.1 broadcast_bitcast_fusion
  34.2 36.6 %shard_map.118.rows_ref = bf16[2048,2304]{1,0:T(8,128)(2,1)S(1)} custom-call(s32[2048]{0:T(1024)S(1)} %add_select_fusion.index_ref, bf16[1024,8,2304]{2,1,0:T(8,128)(2,1)} %bitcast.99), custom_call_target="tpu_custom_call" | custom-call | flops 75497472 | bytes 84934656 | tf_op jit(solution)/shard_map/pallas_call | solution.py:61
  70.9 3.6 %copy-done.2 = bf16[2048,2304]{1,0:T(8,128)(2,1)} copy-done((bf16[2048,2304]{1,0:T(8,128)(2,1)}, bf16[2048,2304]{1,0:T(8,128)(2,1)S(1)}, u32[]{:S(2)}) %copy-start.2) | copy-done | bytes 9437208
  74.5 0.1 fusion.23.token_ref
  74.6 11.5 %all-to-all-done.1 = bf16[8,264,256]{2,1,0:T(8,128)(2,1)S(1)} async-done(((bf16[8,264,256]{2,1,0:T(8,128)(2,1)}), bf16[8,264,256]{2,1,0:T(8,128)(2,1)S(1)}, u32[]{:S(2)}, u32[]{:S(2)}) %all-to-all-start.1) | async-done | bytes 1081376 | tf_op jit(solution)/shard_map/all_to_all | solution.py:247
  86.1 0.1 slice.56
  86.2 0.1 copy.40
  86.4 0.1 reshape.311
  86.5 0.5 fusion.3.picked_ref
  87.0 0.0 all-gather.5.cloned.1.call-done.values_ref
  87.0 12.8 %shard_map.119.more_0_ = f32[256,2048]{1,0:T(8,128)S(1)} custom-call(bf16[2048,2304]{1,0:T(8,128)(2,1)} %copy-done.2, bf16[512,2304]{1,0:T(8,128)(2,1)} %all-gather.5.cloned.1.call-done.values_ref, bf16[8,256,256]{2,1,0:T(8,128)(2,1)S(1)} %bitcast.96, bf16[16,256,32]{2,1,0:T(8,128)(2,1)S(1)} %fusion.3.picked_ref, s32[1,2048]{1,0:T(1,128)S(1)} %fusion.23.token_ref), custom_call_target="tpu_custom_call" | custom-call | flops 6979321856 | bytes 9437184 | tf_op jit(solution)/shard_map/pallas_call | solution.py:114
  99.8 0.0 copy-start.3
  99.8 1.4 copy-done.3
  101.2 35.9 %all-gather.3.cloned.1.call-done.values_ref = bf16[512,2304]{1,0:T(8,128)(2,1)} async-done(((bf16[128,2304]{1,0:T(8,128)(2,1)}), bf16[512,2304]{1,0:T(8,128)(2,1)}) %all-gather.3.cloned.1.call-update) | async-done | bytes 2359312 | tf_op jit(solution)/shard_map/all_gather | solution.py:184
  137.2 1.6 copy-done.4
  138.8 12.8 %shard_map.120 = bf16[256,2048]{1,0:T(8,128)(2,1)S(1)} custom-call(bf16[2048,2304]{1,0:T(8,128)(2,1)} %copy-done.2, bf16[512,2304]{1,0:T(8,128)(2,1)} %all-gather.3.cloned.1.call-done.values_ref, bf16[8,256,256]{2,1,0:T(8,128)(2,1)S(1)} %bitcast.97, bf16[16,256,32]{2,1,0:T(8,128)(2,1)S(1)} %fusion.3.picked_ref, s32[1,2048]{1,0:T(1,128)S(1)} %fusion.23.token_ref, ...), custom_call_target="tpu_custom_call" | custom-call | flops 6979321856 | bytes 9437184 | tf_op jit(solution)/shard_map/pallas_call | solution.py:114
  151.6 0.0 slice-start
  151.6 0.0 copy-start.8
  151.6 0.0 copy-start.9
  151.7 1.5 collective-permute-start.1
  153.2 12.2 %collective-permute-done.1 = bf16[128,2048]{1,0:T(8,128)(2,1)S(1)} collective-permute-done((bf16[128,2048]{1,0:T(8,128)(2,1)S(1)}, bf16[128,2048]{1,0:T(8,128)(2,1)S(1)}, u32[]{:S(2)}, u32[]{:S(2)}) %collective-permute-start.1) | collective-permute-done | bytes 524320 | tf_op jit(solution)/shard_map/ppermute | solution.py:176
  165.3 0.1 add_convert_fusion
  165.5 0.3 copy.45
  165.8 1.0 copy.46
  166.8 3.5 %all-to-all-start.2 = ((bf16[4,128,512]{2,1,0:T(8,128)(2,1)}), bf16[4,128,512]{2,1,0:T(8,128)(2,1)S(1)}, u32[]{:S(2)}, u32[]{:S(2)}) async-start(bf16[4,128,512]{2,1,0:T(8,128)(2,1)} %bitcast.27), calls=%async_computation.2 | async-start | bytes 1048576 | tf_op jit(solution)/shard_map/all_to_all | solution.py:291
  170.3 0.1 fusion.33
  170.4 0.1 fusion.31
  170.4 13.6 %all-to-all-done.2.replies_ref = bf16[4,128,512]{2,1,0:T(8,128)(2,1)S(1)} async-done(((bf16[4,128,512]{2,1,0:T(8,128)(2,1)}), bf16[4,128,512]{2,1,0:T(8,128)(2,1)S(1)}, u32[]{:S(2)}, u32[]{:S(2)}) %all-to-all-start.2) | async-done | bytes 524320 | tf_op jit(solution)/shard_map/all_to_all | solution.py:291
  184.1 1.4 shard_map.121
  185.5 0.0 copy-done.1
  (32 shorter events, 0.3 us)
Async XLA Ops:
  6.5 3.6 %copy-start = (bf16[1,512,2304]{2,1,0:T(8,128)(2,1)S(1)}, bf16[1,512,2304]{2,1,0:T(8,128)(2,1)}, u32[]{:S(2)}) copy-start(bf16[1,512,2304]{2,1,0:T(8,128)(2,1)} %param.14) | copy-start | bytes 7077892
  6.5 80.5 %all-gather.5.cloned.1.call-start = ((), (), s32[]{:S(2)}) async-start(), calls=%async_computation.4 | async-start | bytes 2949120 | tf_op jit(solution)/shard_map/all_gather | solution.py:184
  10.1 127.1 %all-gather.3.cloned.1.call-start = ((), (), s32[]{:S(2)}) async-start(), calls=%async_computation.3 | async-start | bytes 2949120 | tf_op jit(solution)/shard_map/all_gather | solution.py:184
  10.2 5.2 %copy-start.5 = (s32[1024,1]{0,1:T(1,128)S(1)}, s32[1024,1]{0,1:T(1,128)}, u32[]{:S(2)}) copy-start(s32[1024,1]{0,1:T(1,128)} %param.20) | copy-start | bytes 12292
  10.2 6.9 %copy-start.7 = (s32[1024]{0:T(1024)S(1)}, s32[1024]{0:T(1024)}, u32[]{:S(2)}) copy-start(s32[1024]{0:T(1024)} %param.21) | copy-start | bytes 12292
  10.2 13.3 %copy-start.6 = (f32[1,16,8,32]{3,2,1,0:T(8,128)S(1)}, f32[1,16,8,32]{3,2,1,0:T(8,128)}, u32[]{:S(2)}) copy-start(f32[1,16,8,32]{3,2,1,0:T(8,128)} %param.17) | copy-start | bytes 49156
  10.2 13.4 %copy-start.10 = (s32[1,256]{1,0:T(1,128)S(1)}, s32[1,256]{1,0:T(1,128)}, u32[]{:S(2)}) copy-start(s32[1,256]{1,0:T(1,128)} %param.16) | copy-start | bytes 3076
  10.2 13.4 %copy-start.11 = (f32[1,3,32]{2,0,1:T(1,128)S(1)}, f32[1,3,32]{2,0,1:T(1,128)}, u32[]{:S(2)}) copy-start(f32[1,3,32]{2,0,1:T(1,128)} %param.19) | copy-start | bytes 1156
  12.4 11.4 %collective-permute-start = (f32[128,512]{1,0:T(8,128)S(1)}, f32[128,512]{1,0:T(8,128)S(1)}, u32[]{:S(2)}, u32[]{:S(2)}) collective-permute-start(f32[128,512]{1,0:T(8,128)S(1)} %constant_dynamic-slice_fusion.1), channel_id=1, source_target_pairs={{0,2},{2,0},{1,3},{3,1},{4,6},{6,4},{5,7},{7,5},{8,10},{10,8},{9,1... | collective-permute-start | bytes 786440 | tf_op jit(solution)/shard_map/ppermute | solution.py:176
  18.6 10.6 %all-to-all-start = ((s32[4,1,512]{2,1,0:T(1,128)}), s32[4,1,512]{2,1,0:T(1,128)S(1)}, u32[]{:S(2)}, u32[]{:S(2)}) async-start(s32[4,1,512]{2,1,0:T(1,128)} %bitcast.3), calls=%async_computation | async-start | bytes 16384 | tf_op jit(solution)/shard_map/all_to_all | solution.py:203
  30.3 55.8 %all-to-all-start.1 = ((bf16[8,264,256]{2,1,0:T(8,128)(2,1)}), bf16[8,264,256]{2,1,0:T(8,128)(2,1)S(1)}, u32[]{:S(2)}, u32[]{:S(2)}) async-start(bf16[8,264,256]{2,1,0:T(8,128)(2,1)} %broadcast_in_dim.51), calls=%async_computation.1 | async-start | bytes 2162688 | tf_op jit(solution)/shard_map/all_to_all | solution.py:247
  70.9 3.6 %copy-start.2 = (bf16[2048,2304]{1,0:T(8,128)(2,1)}, bf16[2048,2304]{1,0:T(8,128)(2,1)S(1)}, u32[]{:S(2)}) copy-start(bf16[2048,2304]{1,0:T(8,128)(2,1)S(1)} %shard_map.118.rows_ref) | copy-start | bytes 28311556
  99.8 1.5 copy-start.3
  137.2 1.6 copy-start.4
  151.6 18.6 %slice-start = ((f32[1,3,32]{2,0,1:T(1,128)}), f32[1,1,32]{2,0,1:T(1,128)S(1)}, s32[]{:S(2)}) async-start(f32[1,3,32]{2,0,1:T(1,128)} %param.19), calls=%async_computation.5 | async-start | bytes 1024 | tf_op jit(solution)/shard_map/slice | solution.py:299
  151.6 18.7 %copy-start.8 = (f32[1024]{0:T(1024)S(1)}, f32[1024]{0:T(1024)}, u32[]{:S(2)}) copy-start(f32[1024]{0:T(1024)} %param.22) | copy-start | bytes 12292
  151.6 18.7 %copy-start.9 = (s32[1024]{0:T(1024)S(1)}, s32[1024]{0:T(1024)}, u32[]{:S(2)}) copy-start(s32[1024]{0:T(1024)} %param.23) | copy-start | bytes 12292
  151.7 13.7 %collective-permute-start.1 = (bf16[128,2048]{1,0:T(8,128)(2,1)S(1)}, bf16[128,2048]{1,0:T(8,128)(2,1)S(1)}, u32[]{:S(2)}, u32[]{:S(2)}) collective-permute-start(bf16[128,2048]{1,0:T(8,128)(2,1)S(1)} %constant_dynamic-slice_fusion), channel_id=1, source_target_pairs={{0,2},{2,0},{1,3},{3,1},{4,6},{6,4},{5,7},{7,5},{8,10},{10,8},{9,1... | collective-permute-start | bytes 1572872 | tf_op jit(solution)/shard_map/ppermute | solution.py:176
  165.3 20.2 %copy-start.1 = (bf16[1,512,2304]{2,1,0:T(8,128)(2,1)S(1)}, bf16[1,512,2304]{2,1,0:T(8,128)(2,1)}, u32[]{:S(2)}) copy-start(bf16[1,512,2304]{2,1,0:T(8,128)(2,1)} %param.14) | copy-start | bytes 7077892
  166.8 17.3 %all-to-all-start.2 = ((bf16[4,128,512]{2,1,0:T(8,128)(2,1)}), bf16[4,128,512]{2,1,0:T(8,128)(2,1)S(1)}, u32[]{:S(2)}, u32[]{:S(2)}) async-start(bf16[4,128,512]{2,1,0:T(8,128)(2,1)} %bitcast.27), calls=%async_computation.2 | async-start | bytes 1048576 | tf_op jit(solution)/shard_map/all_to_all | solution.py:291
Sparse Core Ops, SparseCore 0:
  10.2 76.1 all-gather.4
  88.0 49.1 all-gather.2
